TPU v7x, 256 devices: a whole 4x4x8 slice. The times are simulated.
256 devices in a mesh: dp: 32 (over z_hi, x, core), tensor: 8 (over y, z_lo).
Axes of the slice: x: 4, y: 4, z: 8 (z_hi: 4, z_lo: 2; z = z_hi * 2 + z_lo), core: 2. Of those that a mesh axis runs over, the one named last changes fastest.
Arguments:
- queries: bfloat16 [8192, 7680], P('dp', 'tensor'), may hold values from -16 to 16
- keys_values: bfloat16 [8192, 1024], P('dp', 'tensor'), may hold values from -16 to 16
- out_weight: bfloat16 [7424, 7680], P('dp', 'tensor'), may hold values from -0.0625 to 0.0625
- cotangent: bfloat16 [8192, 7424], P('dp', 'tensor'), may hold values from -6 to 6
Outputs:
- block_out: bfloat16 [8192, 7424], P('dp', 'tensor')
- grad_queries: bfloat16 [8192, 7680], P('dp', 'tensor')
- grad_keys_values: bfloat16 [8192, 1024], P('dp', 'tensor')
- grad_out_weight: bfloat16 [7424, 7680], P('dp', 'tensor')
All inputs are finite; a program needn't handle non-finite values.
Results may differ from a plain program's by a relative error of at most 0.024.
Values may be sent and summed in bfloat16 or wider, within the bound.
A program may use at most 128 MiB of HBM per device.

v0:
```python
import math

import jax
import jax.numpy as jnp
from jax import lax
from jax.sharding import PartitionSpec as P

HD = 64


masked_score = -1e30


def softmax_rows(q_local, kv_local):
    length = q_local.shape[0]
    kv_heads = kv_local.shape[1] // (2 * HD)
    groups = q_local.shape[1] // (HD * kv_heads)
    scaling = 1.0 / math.sqrt(HD)
    q_heads = q_local.reshape(length, kv_heads, groups, HD)
    kv_pairs = kv_local.reshape(length, kv_heads, 2, HD)
    key_rows = kv_pairs[:, :, 0]
    value_rows = kv_pairs[:, :, 1]
    scores = (
        jnp.einsum("ikgd,jkd->kgij", q_heads, key_rows, preferred_element_type=jnp.float32)
        * scaling
    )
    causal = lax.broadcasted_iota(jnp.int32, (length, length), 0) >= lax.broadcasted_iota(
        jnp.int32, (length, length), 1
    )
    scores = jnp.where(causal, scores, masked_score)
    lifted = jnp.exp(scores - jnp.max(scores, axis=-1, keepdims=True))
    softmax_p = lifted / jnp.sum(lifted, axis=-1, keepdims=True)
    weights = softmax_p.astype(jnp.bfloat16)
    attended = (
        jnp.einsum("kgij,jkd->ikgd", weights, value_rows, preferred_element_type=jnp.float32)
        .astype(jnp.bfloat16)
        .reshape(length, q_local.shape[1])
    )
    return (attended, softmax_p, weights, q_heads, key_rows, value_rows)


def backward_heads(grad_attn, softmax_p, weights, q_heads, key_rows, value_rows):
    length = q_heads.shape[0]
    scaling = 1.0 / math.sqrt(HD)
    grad_heads = grad_attn.reshape(q_heads.shape)
    grad_p = jnp.einsum(
        "ikgd,jkd->kgij", grad_heads, value_rows, preferred_element_type=jnp.float32
    )
    row_dot = jnp.sum(softmax_p * grad_p, axis=-1, keepdims=True)
    grad_scores = (softmax_p * (grad_p - row_dot) * scaling).astype(jnp.bfloat16)
    grad_q = (
        jnp.einsum("kgij,jkd->ikgd", grad_scores, key_rows, preferred_element_type=jnp.float32)
        .astype(jnp.bfloat16)
        .reshape(length, grad_attn.shape[1])
    )
    grad_k = jnp.einsum("kgij,ikgd->jkd", grad_scores, q_heads, preferred_element_type=jnp.float32)
    grad_v = jnp.einsum("kgij,ikgd->jkd", weights, grad_heads, preferred_element_type=jnp.float32)
    grad_kv = (
        jnp.stack([grad_k, grad_v], axis=2)
        .astype(jnp.bfloat16)
        .reshape(length, 2 * key_rows.shape[1] * HD)
    )
    return (grad_q, grad_kv)


def body(queries, keys_values, out_weight, cotangent):
    attended, softmax_p, weights, q_heads, key_rows, value_rows = softmax_rows(queries, keys_values)
    full_cot = lax.all_gather(cotangent, "tensor", axis=1, tiled=True)
    length = attended.shape[0]
    shard_rows = lax.all_gather(out_weight, "dp", axis=0, tiled=True)
    columns = lax.dot_general(
        attended, shard_rows, (((1,), (1,)), ((), ())), preferred_element_type=jnp.float32
    )
    partial_out = columns
    cot_block = full_cot
    grad_sum = jnp.dot(cot_block, shard_rows, preferred_element_type=jnp.float32)
    partial_out, grad_sum = (partial_out, grad_sum)
    block_out = lax.psum_scatter(
        partial_out.astype(jnp.bfloat16), "tensor", scatter_dimension=1, tiled=True
    )
    grad_attn = grad_sum.astype(jnp.bfloat16)
    grad_q, grad_kv = backward_heads(grad_attn, softmax_p, weights, q_heads, key_rows, value_rows)
    inverse = 1.0 / length
    cot_block = full_cot
    grad_weight = lax.psum_scatter(
        (
            lax.dot_general(
                cot_block, attended, (((0,), (0,)), ((), ())), preferred_element_type=jnp.float32
            )
            * inverse
        ).astype(jnp.bfloat16),
        "dp",
        scatter_dimension=0,
        tiled=True,
    )
    return (block_out, grad_q, grad_kv, grad_weight)


def solution(mesh):
    return jax.shard_map(
        body,
        mesh=mesh,
        in_specs=(P("dp", "tensor"), P("dp", "tensor"), P("dp", "tensor"), P("dp", "tensor")),
        out_specs=(P("dp", "tensor"), P("dp", "tensor"), P("dp", "tensor"), P("dp", "tensor")),
        check_vma=False,
    )
```

profile of v0, /device:TPU:1, one launch (start us, length us, event | category | flops | bytes accessed | tf_op | source)
XLA Modules:
  0.0 467.3 jit_solution(12764475621034559859)
XLA Ops:
  7.2 0.7 all-gather.5.cloned.1.call-update
  7.9 0.0 all-gather.3.cloned.1.call-start
  8.0 0.7 all-gather.3.cloned.1.call-update
  8.7 0.0 reduce-scatter.7.cloned.1.call-start
  8.7 0.9 copy.15
  9.7 0.8 fusion.7
  10.5 0.8 fusion.6
  11.3 1.2 copy-done.1
  12.5 1.1 fusion.14
  13.6 85.9 %all-gather.5.cloned.1.call-done = bf16[256,7424]{0,1:T(8,128)(2,1)} async-done(((bf16[256,928]{0,1:T(8,128)(2,1)}), bf16[256,7424]{0,1:T(8,128)(2,1)}) %all-gather.5.cloned.1.call-update) | async-done | bytes 3801104 | tf_op jit(solution)/shard_map/all_gather | solution.py:68
  99.5 9.2 %fusion = bf16[7424,960]{0,1:T(8,128)(2,1)} fusion(bf16[256,960]{0,1:T(8,128)(2,1)S(1)} %bitcast.137, bf16[256,7424]{0,1:T(8,128)(2,1)} %all-gather.5.cloned.1.call-done), kind=kOutput, calls=%fused_computation.1 | convolution fusion | flops 3663298560 | bytes 18546688 | tf_op jit(solution)/shard_map/dot_general | solution.py:87
  108.7 20.0 %copy.26 = bf16[7424,960]{1,0:T(8,128)(2,1)} copy(bf16[7424,960]{0,1:T(8,128)(2,1)} %fusion) | data formatting | bytes 28508160
  128.7 0.2 reduce-scatter.5.cloned.1.call-start
  129.0 77.8 %all-gather.3.cloned.1.call-done = bf16[7424,960]{1,0:T(8,128)(2,1)} async-done(((bf16[232,960]{1,0:T(8,128)(2,1)}), bf16[7424,960]{1,0:T(8,128)(2,1)}) %all-gather.3.cloned.1.call-update) | async-done | bytes 14254096 | tf_op jit(solution)/shard_map/all_gather | solution.py:70
  206.7 11.3 %convolution_convert_fusion = bf16[256,7424]{0,1:T(8,128)(2,1)} fusion(bf16[7424,960]{1,0:T(8,128)(2,1)} %all-gather.3.cloned.1.call-done, bf16[256,960]{0,1:T(8,128)(2,1)S(1)} %bitcast.138), kind=kOutput, calls=%fused_computation.2 | convolution fusion | flops 3650945024 | bytes 18546688 | tf_op jit(solution)/shard_map/dot_general | solution.py:71
  218.1 12.4 %convolution_convert_fusion.1 = bf16[256,960]{0,1:T(8,128)(2,1)S(1)} fusion(bf16[256,7424]{0,1:T(8,128)(2,1)} %all-gather.5.cloned.1.call-done, bf16[7424,960]{1,0:T(8,128)(2,1)} %all-gather.3.cloned.1.call-done), kind=kOutput, calls=%fused_computation.20 | convolution fusion | flops 3649290240 | bytes 18546688 | tf_op jit(solution)/shard_map/dot_general | solution.py:76
  230.5 1.4 fusion.1
  231.9 1.4 fusion.8
  233.3 0.7 fusion.27
  234.1 1.1 fusion.24
  235.2 0.7 copy.20
  235.9 3.0 convolution_convert_fusion.2
  238.9 131.8 %reduce-scatter.7.cloned.1.call-done = bf16[232,960]{1,0:T(8,128)(2,1)} async-done(((bf16[7424,960]{1,0:T(8,128)(2,1)}), bf16[232,960]{1,0:T(8,128)(2,1)}) %reduce-scatter.7.cloned.1.call-update) | async-done | bytes 445456
  370.7 90.0 %reduce-scatter.5.cloned.1.call-done = bf16[256,928]{0,1:T(8,128)(2,1)} async-done(((bf16[256,7424]{0,1:T(8,128)(2,1)}), bf16[256,928]{0,1:T(8,128)(2,1)}) %reduce-scatter.5.cloned.1.call-update) | async-done | bytes 475152 | tf_op jit(solution)/shard_map/reduce_scatter | solution.py:78
  (12 shorter events, 0.1 us)
Async XLA Ops:
  7.2 2.5 copy-start
  7.2 92.3 %all-gather.5.cloned.1.call-start = ((), (), s32[]{:S(2)}) async-start(), calls=%async_computation.4 | async-start | bytes 4276224 | tf_op jit(solution)/shard_map/all_gather | solution.py:68
  7.9 198.8 %all-gather.3.cloned.1.call-start = ((), (), s32[]{:S(2)}) async-start(), calls=%async_computation.2 | async-start | bytes 15679488 | tf_op jit(solution)/shard_map/all_gather | solution.py:70
  8.7 362.1 %reduce-scatter.7.cloned.1.call-start = ((), (), s32[]{:S(2)}) async-start(), calls=%async_computation.5 | async-start | bytes 15679488
  10.5 2.0 copy-start.1
  128.7 332.0 %reduce-scatter.5.cloned.1.call-start = ((), (), s32[]{:S(2)}) async-start(), calls=%async_computation.3 | async-start | bytes 4276224 | tf_op jit(solution)/shard_map/reduce_scatter | solution.py:78
  218.1 12.4 %copy-start.2 = (f32[256,256,15]{1,0,2:T(8,128)S(1)}, f32[256,256,15]{1,0,2:T(8,128)}, u32[]{:S(2)}) copy-start(f32[256,256,15]{1,0,2:T(8,128)} %copy-done.1) | copy-start | bytes 11796484
  233.3 1.9 copy-start.3
Sparse Core Ops, SparseCore 0:
  9.8 89.6 all-gather.4
  102.1 104.6 all-gather.2
  211.5 159.1 reduce-scatter.6
  373.9 86.7 reduce-scatter.4
where the time goes:
time: 468 us; the launch traced here: 467 us
  waiting for transfers between devices  387 us (83%)
  matrix products  41 us (9%)
  local copies, waits for them, and re-layouts  22.9 us (5%)
  between operations  13.9 us (3%)
    unnamed x5, waiting for transfers between devices  133 us
    reduce_scatter x1, waiting for transfers between devices, body(): lax.psum_scatter(partial_out.astype(jnp.bfloat16), 'tensor', scatter_dime...  90 us
    all_gather x1, waiting for transfers between devices, body(): full_cot = lax.all_gather(cotangent, 'tensor', axis=1, tiled=True)  85.9 us
    all_gather x1, waiting for transfers between devices, body(): shard_rows = lax.all_gather(out_weight, 'dp', axis=0, tiled=True)  77.8 us
    unnamed x11, local copies, waits for them, and re-layouts  22.9 us
    dot_general x1, matrix products, body(): jnp.dot(cot_block, shard_rows, preferred_element_type=jnp.float32)  12.4 us
    dot_general x1, matrix products, body(): lax.dot_general(attended, shard_rows, (((1,), (1,)), ((), ())), preferred...  11.3 us
  transfers between devices with their start and end apart: 4, of which 4 were waited for; matrix products, arithmetic and copies ran while one was open for 14% of the time, Pallas kernels for 0%

commit v1 on v0

v1 whole, which is shorter than its diff:
```python
import functools
import math

import jax
import jax.numpy as jnp
from jax import lax
from jax.experimental import pallas as pl
from jax.experimental.pallas import tpu as pltpu
from jax.sharding import PartitionSpec as P

MESH = pl.DeviceIdType.MESH
HD = 64
HEADS = 15
TOK = 256
HCOL = HEADS * HD
ROWS = 232
PAD = 240
SEGMENT = 5
MASKED = -1e30
BF = jnp.bfloat16
F32 = jnp.float32


def device(zh, x, c, y, zl):
    return (zh * 8 + x * 2 + c, y * 2 + zl)


def kernel(
    q_t, kv, kv_t, w_in, cot_in,
    out_o, gq_o, gkv_o, gw_o,
    cz, cot_all, w_all, att_all, probs, w_t,
    o_part, o_recv, rx, rz, g_part, g_core, g_recv, a_part, a_recv, gkv_acc,
    zl_s, zl_r, xa_s, xa_r, yg_s, yg_r, zg_s, zg_r, wc_s, wc_r, xg_s, xg_r,
    yr_s, yr_r, xo_s, xo_r, zo_s, zo_r, gc_s, gc_r, zr_s, zr_r, ar_s, ar_r,
):
    dp = lax.axis_index("dp")
    tensor = lax.axis_index("tensor")
    zh, x, c = dp // 8, (dp // 2) % 4, dp % 2
    y, zl = tensor // 2, tensor % 2
    sign = 1 - 2 * c
    x_p, x_m, x_2 = (x + 4 + sign) % 4, (x + 4 - sign) % 4, (x + 2) % 4
    y_p, y_m, y_2 = (y + 4 + sign) % 4, (y + 4 - sign) % 4, (y + 2) % 4
    z_p, z_m, z_2 = (zh + 4 + sign) % 4, (zh + 4 - sign) % 4, (zh + 2) % 4
    at_x = lambda other: device(zh, other, c, y, zl)
    at_y = lambda other: device(zh, x, c, other, zl)
    at_z = lambda other: device(other, x, c, y, zl)
    sibling = device(zh, x, 1 - c, y, zl)
    partner = device(zh, x, c, y, 1 - zl)

    def send(src, dst, send_sem, recv_sem, to):
        return pltpu.make_async_remote_copy(
            src_ref=src, dst_ref=dst, send_sem=send_sem, recv_sem=recv_sem,
            device_id=to, device_id_type=MESH,
        )

    started = []

    def start(*args):
        copy = send(*args)
        copy.start()
        started.append(copy)
        return copy

    barrier = pltpu.get_barrier_semaphore()
    others = [sibling, partner, at_x(x_p), at_x(x_m), at_x(x_2)]
    others += [at_y(y_p), at_y(y_m), at_z(z_p), at_z(z_m)]
    for other in others:
        pl.semaphore_signal(barrier, inc=1, device_id=other, device_id_type=MESH)
    pl.semaphore_wait(barrier, len(others))

    zl_copy = start(cot_in, cz.at[zl], zl_s.at[0], zl_r.at[0], partner)
    cz[zl] = cot_in[...]
    w_all[zh, c] = w_in[...]

    row = lax.broadcasted_iota(jnp.int32, (TOK, TOK), 0)
    col = lax.broadcasted_iota(jnp.int32, (TOK, TOK), 1)
    allowed = row <= col
    scale = 1.0 / math.sqrt(HD)

    def forward_head(h, carry):
        rows = pl.ds(pl.multiple_of(h * HD, HD), HD)
        scores = jnp.dot(kv[:, :HD], q_t[rows, :], preferred_element_type=F32)
        scores = jnp.where(allowed, scores * scale, MASKED)
        lifted = jnp.exp(scores - jnp.max(scores, axis=0, keepdims=True))
        soft = lifted / jnp.sum(lifted, axis=0, keepdims=True)
        probs[h] = soft
        attended = jnp.dot(kv_t[HD:, :], soft.astype(BF), preferred_element_type=F32)
        att_all[x, rows, :] = attended.astype(BF)
        return carry

    att_copies = []

    def attention_segment(k):
        lax.fori_loop(k * SEGMENT, (k + 1) * SEGMENT, forward_head, 0)
        part = att_all.at[x, pl.ds(k * SEGMENT * HD, SEGMENT * HD)]
        first = start(part, part, xg_s.at[0, k], xg_r.at[0, k], at_x(x_p))
        second = start(part, part, xg_s.at[1, k], xg_r.at[1, k], at_x(x_m))
        att_copies.append((first, second))

    attention_segment(0)
    attention_segment(1)

    zl_copy.wait_recv()
    w_p = start(w_in, w_all.at[zh, c], zg_s.at[0], zg_r.at[0], at_z(z_p))
    w_m = start(w_in, w_all.at[zh, c], zg_s.at[1], zg_r.at[1], at_z(z_m))
    w_c = [start(w_in, w_all.at[zh, c], wc_s.at[0], wc_r.at[0], sibling)]
    xa = []
    for d in (1, 2, 3):
        to = (x + d) % 4
        piece = cz.at[to // 2, pl.ds(2 * (to % 2), 2)]
        xa.append(start(piece, cot_all.at[y, x], xa_s.at[d - 1], xa_r.at[d - 1], at_x(to)))
    cot_all[y, x] = cz[x // 2, pl.ds(2 * (x % 2), 2)]

    attention_segment(2)

    yg = []

    def y_start(k, j):
        block = cot_all.at[y, j]
        first = start(block, block, yg_s.at[0, k], yg_r.at[0, k], at_y(y_p))
        second = start(block, block, yg_s.at[1, k], yg_r.at[1, k], at_y(y_m))
        yg.append((first, second))

    y_start(0, x)
    for k in (1, 3, 2):
        xa[k - 1].wait_recv()
        y_start(k, (x + 4 - k) % 4)

    forwarded = []
    for k in range(3):
        att_copies[k][0].wait_recv()
        part = att_all.at[x_m, pl.ds(k * SEGMENT * HD, SEGMENT * HD)]
        forwarded.append(start(part, part, xg_s.at[2, k], xg_r.at[2, k], at_x(x_p)))

    w_p.wait_recv()
    block = w_all.at[z_m, c]
    w_f = start(block, block, zg_s.at[2], zg_r.at[2], at_z(z_p))
    w_c.append(start(block, block, wc_s.at[1], wc_r.at[1], sibling))
    w_m.wait_recv()
    block = w_all.at[z_p, c]
    w_c.append(start(block, block, wc_s.at[2], wc_r.at[2], sibling))

    yf = []
    for i, k in enumerate((0, 1, 3, 2)):
        yg[i][0].wait_recv()
        block = cot_all.at[y_m, (x + 4 - k) % 4]
        yf.append(start(block, block, yg_s.at[2, k], yg_r.at[2, k], at_y(y_p)))

    for k in range(3):
        att_copies[k][1].wait_recv()
        forwarded[k].wait_recv()
    w_f.wait_recv()
    block = w_all.at[z_2, c]
    w_c.append(start(block, block, wc_s.at[3], wc_r.at[3], sibling))
    for copy in w_c:
        copy.wait_recv()

    def out_partial(dest):
        weight = w_all[dest].reshape(2 * PAD, HCOL)

        def one(j, carry):
            value = jnp.dot(weight, att_all[j], preferred_element_type=F32)
            o_part[dest, j] = value.astype(BF).reshape(2, PAD, TOK)
            return carry

        lax.fori_loop(0, 4, one, 0)

    out_partial(y_2)
    yr0 = [start(o_part.at[y_2, j], o_recv.at[0, j], yr_s.at[0, j], yr_r.at[0, j], at_y(y_m)) for j in range(4)]
    out_partial(y_p)
    yr1 = [start(o_part.at[y_p, j], o_recv.at[1, j], yr_s.at[1, j], yr_r.at[1, j], at_y(y_p)) for j in range(4)]
    out_partial(y_m)
    out_partial(y)

    def transpose_weight(k, carry):
        w_t[k] = jnp.transpose(w_all[k].reshape(2 * PAD, HCOL))
        return carry

    lax.fori_loop(0, 4, transpose_weight, 0)

    for i in range(4):
        yg[i][1].wait_recv()
        yf[i].wait_recv()

    def weight_partial(dest):
        total = jnp.zeros((2 * PAD, HCOL), F32)
        for j in range(4):
            total += lax.dot_general(
                cot_all[dest, j].reshape(2 * PAD, TOK), att_all[j],
                (((1,), (1,)), ((), ())), preferred_element_type=F32,
            )
        g_part[dest] = (total * (1.0 / TOK)).astype(BF).reshape(2, PAD, HCOL)

    gc = []

    def weight_step(k, dest):
        weight_partial(dest)
        gc.append(start(g_part.at[dest, 1 - c], g_core.at[dest], gc_s.at[dest], gc_r.at[dest], sibling))

    def attended_partial(dest):
        total = jnp.zeros((HCOL, TOK), F32)
        for k in range(4):
            total += jnp.dot(w_t[k], cot_all[k, dest].reshape(2 * PAD, TOK), preferred_element_type=F32)
        a_part[dest] = total.astype(BF)

    def add_out(dest, kind, j):
        value = o_part[dest, j].astype(F32) + o_recv[kind, j].astype(F32)
        o_part[dest, j] = value.astype(BF)

    attended_partial(x_2)
    ar0 = start(a_part.at[x_2], a_recv.at[0], ar_s.at[0], ar_r.at[0], at_x(x_m))
    weight_step(0, z_2)
    yr2 = []
    for j in range(4):
        yr0[j].wait_recv()
        add_out(y_m, 0, j)
        yr2.append(start(o_part.at[y_m, j], o_recv.at[2, j], yr_s.at[2, j], yr_r.at[2, j], at_y(y_m)))
    attended_partial(x_p)
    ar1 = start(a_part.at[x_p], a_recv.at[1], ar_s.at[1], ar_r.at[1], at_x(x_p))
    attended_partial(x_m)
    ar0.wait_recv()
    a_part[x_m] = (a_part[x_m].astype(F32) + a_recv[0].astype(F32)).astype(BF)
    ar2 = start(a_part.at[x_m], a_recv.at[2], ar_s.at[2], ar_r.at[2], at_x(x_m))

    def weight_join(k, dest):
        gc[k].wait_recv()
        g_part[dest, c] = (g_part[dest, c].astype(F32) + g_core[dest].astype(F32)).astype(BF)

    weight_join(0, z_2)
    zr0 = start(g_part.at[z_2, c], g_recv.at[0], zr_s.at[0], zr_r.at[0], at_z(z_m))
    weight_step(1, z_p)
    weight_step(2, z_m)
    weight_join(1, z_p)
    zr1 = start(g_part.at[z_p, c], g_recv.at[1], zr_s.at[1], zr_r.at[1], at_z(z_p))
    weight_step(3, zh)
    attended_partial(x)
    weight_join(2, z_m)
    zr0.wait_recv()
    g_part[z_m, c] = (g_part[z_m, c].astype(F32) + g_recv[0].astype(F32)).astype(BF)
    zr2 = start(g_part.at[z_m, c], g_recv.at[2], zr_s.at[2], zr_r.at[2], at_z(z_m))

    ar1.wait_recv()
    ar2.wait_recv()
    a_part[x] = (
        a_part[x].astype(F32) + a_recv[1].astype(F32) + a_recv[2].astype(F32)
    ).astype(BF)

    gkv_acc[...] = jnp.zeros_like(gkv_acc)

    def backward_head(h, carry):
        rows = pl.ds(pl.multiple_of(h * HD, HD), HD)
        grad = a_part[x, rows, :]
        soft = probs[h]
        grad_p = jnp.dot(kv[:, HD:], grad, preferred_element_type=F32)
        dot = jnp.sum(soft * grad_p, axis=0, keepdims=True)
        grad_s = (soft * (grad_p - dot) * scale).astype(BF)
        gq_o[rows, :] = jnp.dot(kv_t[:HD, :], grad_s, preferred_element_type=F32).astype(BF)
        last = (((1,), (1,)), ((), ()))
        gkv_acc[:HD, :] += lax.dot_general(q_t[rows, :], grad_s, last, preferred_element_type=F32)
        gkv_acc[HD:, :] += lax.dot_general(grad, soft.astype(BF), last, preferred_element_type=F32)
        return carry

    lax.fori_loop(0, 8, backward_head, 0)

    def out_final(j):
        value = o_part[y, j].astype(F32) + o_recv[1, j].astype(F32) + o_recv[2, j].astype(F32)
        return value.astype(BF)

    for j in range(4):
        yr1[j].wait_recv()
        yr2[j].wait_recv()
    xo = []
    for d in (2, 1, 3):
        to = (x + d) % 4
        o_part[y, to] = out_final(to)
        xo.append(start(o_part.at[y, to], rx.at[x], xo_s.at[d - 1], xo_r.at[d - 1], at_x(to)))
    rx[x] = out_final(x)

    lax.fori_loop(8, HEADS, backward_head, 0)
    gkv_o[...] = gkv_acc[...].astype(BF)

    for copy in xo:
        copy.wait_recv()
    zo = start(rx.at[pl.ds(2 * (1 - zl), 2)], rz, zo_s.at[0], zo_r.at[0], partner)

    weight_join(3, zh)
    zr1.wait_recv()
    zr2.wait_recv()
    gw_o[...] = (
        g_part[zh, c].astype(F32) + g_recv[1].astype(F32) + g_recv[2].astype(F32)
    ).astype(BF)

    zo.wait_recv()
    for h in range(2):
        value = rx[2 * zl + h].astype(F32) + rz[h].astype(F32)
        out_o[pl.ds(2 * h, 2)] = value.astype(BF)
    for copy in started:
        copy.wait_send()


def body(queries, keys_values, out_weight, cotangent):
    q_t = queries.T
    kv_t = keys_values.T
    w_in = jnp.pad(out_weight, ((0, PAD - ROWS), (0, 0)))
    cot = jnp.pad(cotangent.T.reshape(4, ROWS, TOK), ((0, 0), (0, PAD - ROWS), (0, 0)))
    vmem = pl.BlockSpec(memory_space=pltpu.VMEM)
    dma = lambda *shape: pltpu.SemaphoreType.DMA(shape)
    scratch = [
        pltpu.VMEM((2, 4, PAD, TOK), BF),
        pltpu.VMEM((4, 4, 2, PAD, TOK), BF),
        pltpu.VMEM((4, 2, PAD, HCOL), BF),
        pltpu.VMEM((4, HCOL, TOK), BF),
        pltpu.VMEM((HEADS, TOK, TOK), F32),
        pltpu.VMEM((4, HCOL, 2 * PAD), BF),
        pltpu.VMEM((4, 4, 2, PAD, TOK), BF),
        pltpu.VMEM((3, 4, 2, PAD, TOK), BF),
        pltpu.VMEM((4, 2, PAD, TOK), BF),
        pltpu.VMEM((2, 2, PAD, TOK), BF),
        pltpu.VMEM((4, 2, PAD, HCOL), BF),
        pltpu.VMEM((4, PAD, HCOL), BF),
        pltpu.VMEM((3, PAD, HCOL), BF),
        pltpu.VMEM((4, HCOL, TOK), BF),
        pltpu.VMEM((3, HCOL, TOK), BF),
        pltpu.VMEM((2 * HD, TOK), F32),
        dma(1), dma(1), dma(3), dma(3), dma(3, 4), dma(3, 4), dma(3), dma(3), dma(4), dma(4),
        dma(3, 3), dma(3, 3), dma(3, 4), dma(3, 4), dma(3), dma(3), dma(1), dma(1),
        dma(4), dma(4), dma(3), dma(3), dma(3), dma(3),
    ]
    out, gq, gkv, gw = pl.pallas_call(
        kernel,
        out_shape=(
            jax.ShapeDtypeStruct((4, PAD, TOK), BF),
            jax.ShapeDtypeStruct((HCOL, TOK), BF),
            jax.ShapeDtypeStruct((2 * HD, TOK), BF),
            jax.ShapeDtypeStruct((PAD, HCOL), BF),
        ),
        in_specs=[vmem] * 5,
        out_specs=(vmem,) * 4,
        scratch_shapes=scratch,
        compiler_params=pltpu.CompilerParams(
            collective_id=0, has_side_effects=True, vmem_limit_bytes=60 * 2**20
        ),
        cost_estimate=pl.CostEstimate(flops=12 * 10**9, bytes_accessed=5 * 10**6, transcendentals=10**6),
    )(q_t, keys_values, kv_t, w_in, cot)
    block_out = out[:, :ROWS].reshape(4 * ROWS, TOK).T
    return block_out, gq.T, gkv.T, gw[:ROWS]


def solution(mesh):
    spec = P("dp", "tensor")
    return jax.shard_map(
        body, mesh=mesh, in_specs=(spec,) * 4, out_specs=(spec,) * 4, check_vma=False
    )
```

time: 468 us -> 144 us (0.31)
  waiting for transfers between devices: 387 us -> 0 us
  Pallas kernels: 0 us -> 133 us
  matrix products: 41 us -> 0 us
  local copies, waits for them, and re-layouts: 22.9 us -> 8.91 us
  between operations: 13.9 us -> 0.66 us
    all_gather x2 -> x0, waiting for transfers between devices: 164 us -> none  [the longest x1 85.9 us: body(): full_cot = lax.all_gather(cotangent, 'tensor', axis=1, tiled=True)]
    pallas_call x0 -> x1, Pallas kernels: none -> 133 us  [body(): pl.pallas_call(kernel, out_shape=(jax.ShapeDtypeStruct((4, PAD, TOK), BF)...]
    unnamed x5 -> x0, waiting for transfers between devices: 133 us -> none
    reduce_scatter x1 -> x0, waiting for transfers between devices: 90 us -> none  [body(): lax.psum_scatter(partial_out.astype(jnp.bfloat16), 'tensor', scatter_dime...]
    dot_general x9 -> x0, matrix products: 41 us -> none  [the longest x1 12.4 us: body(): jnp.dot(cot_block, shard_rows, preferred_element_type=jnp.float32)]
    unnamed x11, local copies, waits for them, and re-layouts: 22.9 us -> 3.5 us
  transfers between devices with their start and end apart: 4 -> 0, of which waited for: 4 -> 0; matrix products, arithmetic and copies ran while one was open for 14% -> 0% of each run, Pallas kernels for 0% -> 0%
where the time goes in v1:
time: 144 us; the launch traced here: 143 us
  Pallas kernels  133 us (92%)
  local copies, waits for them, and re-layouts  8.91 us (6%)
    pallas_call x1, Pallas kernels, body(): pl.pallas_call(kernel, out_shape=(jax.ShapeDtypeStruct((4, PAD, TOK), BF)...  133 us
    unnamed x11, local copies, waits for them, and re-layouts  3.5 us

profile of v1, /device:TPU:1, one launch (start us, length us, event | category | flops | bytes accessed | tf_op | source)
XLA Modules:
  0.0 142.9 jit_solution(16958554318164276581)
XLA Ops:
  0.6 1.6 %copy.8 = bf16[256,128]{0,1:T(8,128)(2,1)} copy(bf16[256,128]{1,0:T(8,128)(2,1)} %kv.1) | data formatting | bytes 131072 | tf_op args[1]
  2.2 0.0 copy-start.1
  2.2 1.9 %pad.8.w_in = bf16[240,960]{1,0:T(8,128)(2,1)} pad(bf16[232,960]{1,0:T(8,128)(2,1)} %param.6, bf16[]{:T(256)} %constant.2.clone.1), padding=0_8x0_0 | pad | bytes 906242 | tf_op jit(solution)/shard_map/jit(_pad)/pad | solution.py:304
  4.1 0.0 copy-done.1
  4.1 0.8 pad.9.cot_in
  4.9 133.4 %shard_map.75 = (bf16[4,240,256]{2,1,0:T(8,128)(2,1)}, bf16[960,256]{1,0:T(8,128)(2,1)}, bf16[128,256]{1,0:T(8,128)(2,1)}, bf16[240,960]{1,0:T(8,128)(2,1)}) custom-call(bf16[960,256]{1,0:T(8,128)(2,1)} %bitcast.15, bf16[256,128]{1,0:T(8,128)(2,1)} %kv.1, bf16[128,256]{1,0:T(8,128)(2,1)} %bitcast.14, bf16[240,960]{1,0:T(8,128)(2,1)} %pad.8.w_in, ...), custom_call_target="tpu_custom_call" | custom-call | flops 12000000000 | bytes 5000000 | tf_op jit(solution)/shard_map/pallas_call | solution.py:329
  138.3 0.0 copy-start.3
  138.3 0.0 copy-start.2
  138.3 1.9 %slice.6 = bf16[4,232,256]{2,1,0:T(8,128)(2,1)} slice(bf16[4,240,256]{2,1,0:T(8,128)(2,1)} %get-tuple-element.8), slice={[0:4], [0:232], [0:256]} | slice | bytes 950272 | tf_op jit(solution)/shard_map/slice | solution.py:345
  140.2 0.0 copy-done.3
  140.2 0.7 copy.9
  140.9 0.0 copy-done.2
  140.9 0.0 copy-start
  140.9 0.8 slice.7
  141.8 0.4 copy-done
  142.2 0.8 copy.11
Async XLA Ops:
  2.2 1.9 %copy-start.1 = (bf16[256,928]{0,1:T(8,128)(2,1)S(1)}, bf16[256,928]{0,1:T(8,128)(2,1)}, u32[]{:S(2)}) copy-start(bf16[256,928]{0,1:T(8,128)(2,1)} %param.7) | copy-start | bytes 1425412
  138.3 1.9 %copy-start.3 = (bf16[128,256]{1,0:T(8,128)(2,1)S(1)}, bf16[128,256]{1,0:T(8,128)(2,1)}, u32[]{:S(2)}) copy-start(bf16[128,256]{1,0:T(8,128)(2,1)} %get-tuple-element.10) | copy-start | bytes 196612
  138.3 2.6 %copy-start.2 = (bf16[240,960]{1,0:T(8,128)(2,1)S(1)}, bf16[240,960]{1,0:T(8,128)(2,1)}, u32[]{:S(2)}) copy-start(bf16[240,960]{1,0:T(8,128)(2,1)} %get-tuple-element.11) | copy-start | bytes 1382404
  140.9 1.2 copy-start

commit v2 on v1

v2 whole, which is shorter than its diff:
```python
import functools
import math

import jax
import jax.numpy as jnp
from jax import lax
from jax.experimental import pallas as pl
from jax.experimental.pallas import tpu as pltpu
from jax.sharding import PartitionSpec as P

MESH = pl.DeviceIdType.MESH
HD = 64
HEADS = 15
TOK = 256
HCOL = HEADS * HD
ROWS = 232
PAD = 240
SEGMENT = 5
CHUNK = 80
MASKED = -1e30
BF = jnp.bfloat16
F32 = jnp.float32


def device(zh, x, c, y, zl):
    return (zh * 8 + x * 2 + c, y * 2 + zl)


def kernel(
    q_t, kv, w_in, cot_ref,
    out_o, gq_o, gkv_o, gw_o,
    kv_t, cz, cot_all, w_all, att_all, probs, w_t,
    o_part, o_recv, rx, rz, g_part, g_core, g_recv, a_part, a_recv, gkv_acc,
    wl_s, wl_r, zl_s, zl_r, xa_s, xa_r, yg_s, yg_r, zg_s, zg_r, wc_s, wc_r, xg_s, xg_r,
    yr_s, yr_r, xo_s, xo_r, zo_s, zo_r, gc_s, gc_r, zr_s, zr_r, ar_s, ar_r,
):
    dp = lax.axis_index("dp")
    tensor = lax.axis_index("tensor")
    zh, x, c = dp // 8, (dp // 2) % 4, dp % 2
    y, zl = tensor // 2, tensor % 2
    sign = 1 - 2 * c
    x_p, x_m, x_2 = (x + 4 + sign) % 4, (x + 4 - sign) % 4, (x + 2) % 4
    y_p, y_m, y_2 = (y + 4 + sign) % 4, (y + 4 - sign) % 4, (y + 2) % 4
    z_p, z_m, z_2 = (zh + 4 + sign) % 4, (zh + 4 - sign) % 4, (zh + 2) % 4
    at_x = lambda other: device(zh, other, c, y, zl)
    at_y = lambda other: device(zh, x, c, other, zl)
    at_z = lambda other: device(other, x, c, y, zl)
    sibling = device(zh, x, 1 - c, y, zl)
    partner = device(zh, x, c, y, 1 - zl)

    def send(src, dst, send_sem, recv_sem, to):
        return pltpu.make_async_remote_copy(
            src_ref=src, dst_ref=dst, send_sem=send_sem, recv_sem=recv_sem,
            device_id=to, device_id_type=MESH,
        )

    started = []

    def start(*args):
        copy = send(*args)
        copy.start()
        started.append(copy)
        return copy

    barrier = pltpu.get_barrier_semaphore()
    others = [sibling, partner, at_x(x_p), at_x(x_m), at_x(x_2)]
    others += [at_y(y_p), at_y(y_m), at_z(z_p), at_z(z_m)]
    for other in others:
        pl.semaphore_signal(barrier, inc=1, device_id=other, device_id_type=MESH)
    pl.semaphore_wait(barrier, len(others))

    turned = cot_ref[...].astype(F32)
    zl_copy = []
    for r in range(2):
        for h in range(2):
            first = (2 * h + r) * ROWS
            cz[zl, r, h, pl.ds(PAD - 16, 16)] = jnp.zeros((16, TOK), BF)
            cz[zl, r, h, pl.ds(0, ROWS)] = turned[first : first + ROWS].astype(BF)
        block = cz.at[zl, r]
        zl_copy.append(start(block, block, zl_s.at[r], zl_r.at[r], partner))
    kv_t[...] = jnp.transpose(kv[...])
    w_all[zh, c, pl.ds(PAD - 16, 16)] = jnp.zeros((16, HCOL), BF)
    w_all[zh, c, pl.ds(0, ROWS)] = w_in[...]

    row = lax.broadcasted_iota(jnp.int32, (TOK, TOK), 0)
    col = lax.broadcasted_iota(jnp.int32, (TOK, TOK), 1)
    allowed = row <= col
    scale = 1.0 / math.sqrt(HD)

    def forward_head(h, carry):
        rows = pl.ds(pl.multiple_of(h * HD, HD), HD)
        scores = jnp.dot(kv[:, :HD], q_t[rows, :], preferred_element_type=F32)
        scores = jnp.where(allowed, scores * scale, MASKED)
        lifted = jnp.exp(scores - jnp.max(scores, axis=0, keepdims=True))
        soft = lifted / jnp.sum(lifted, axis=0, keepdims=True)
        probs[h] = soft
        attended = jnp.dot(kv_t[HD:, :], soft.astype(BF), preferred_element_type=F32)
        att_all[x, rows, :] = attended.astype(BF)
        return carry

    def attention_segment(k):
        lax.fori_loop(k * SEGMENT, (k + 1) * SEGMENT, forward_head, 0)

    def a2a_start(r):
        copies = {}
        for d in (2, 1, 3):
            to = (x + d) % 4
            copies[d] = start(
                cz.at[to // 2, r, to % 2], cot_all.at[y, x, r],
                xa_s.at[r, d - 1], xa_r.at[r, d - 1], at_x(to),
            )
        cot_all[y, x, r] = cz[x // 2, r, x % 2]
        return copies

    def y_start(r, d):
        block = cot_all.at[y, (x + 4 - d) % 4, r]
        return (
            start(block, block, yg_s.at[0, r, d], yg_r.at[0, r, d], at_y(y_p)),
            start(block, block, yg_s.at[1, r, d], yg_r.at[1, r, d], at_y(y_m)),
        )

    def y_forward(r, d):
        yg[r, d][0].wait_recv()
        block = cot_all.at[y_m, (x + 4 - d) % 4, r]
        yf.append(start(block, block, yg_s.at[2, r, d], yg_r.at[2, r, d], at_y(y_p)))

    def w_rows(z, i):
        return w_all.at[z, c, pl.ds(i * CHUNK, CHUNK)]

    def w_core(z):
        block = w_all.at[z, c]
        return start(block, block, wc_s.at[z], wc_r.at[z], sibling)

    wg, w_c = [], []

    def w_start():
        for i in range(3):
            block = w_rows(zh, i)
            wg.append((
                start(block, block, zg_s.at[0, i], zg_r.at[0, i], at_z(z_p)),
                start(block, block, zg_s.at[1, i], zg_r.at[1, i], at_z(z_m)),
            ))
        w_c.append(w_core(zh))

    attention_segment(0)
    attention_segment(1)
    yg, yf, xa = {}, [], {}
    zl_copy[0].wait_recv()
    xa[0] = a2a_start(0)
    yg[0, 0] = y_start(0, 0)
    attention_segment(2)
    zl_copy[1].wait_recv()
    xa[1] = a2a_start(1)
    w_start()
    for d in (1, 3, 2):
        xa[0][d].wait_recv()
        yg[0, d] = y_start(0, d)
    yg[1, 0] = y_start(1, 0)
    y_forward(0, 0)
    for d in (1, 3, 2):
        xa[1][d].wait_recv()
        yg[1, d] = y_start(1, d)
        y_forward(0, d)
    att_copies = []
    for k in range(3):
        part = att_all.at[x, pl.ds(k * SEGMENT * HD, SEGMENT * HD)]
        att_copies.append((
            start(part, part, xg_s.at[0, k], xg_r.at[0, k], at_x(x_p)),
            start(part, part, xg_s.at[1, k], xg_r.at[1, k], at_x(x_m)),
        ))
    y_forward(1, 0)
    w_f, forwarded = [], []
    for i, d in enumerate((1, 3, 2)):
        wg[i][0].wait_recv()
        block = w_rows(z_m, i)
        w_f.append(start(block, block, zg_s.at[2, i], zg_r.at[2, i], at_z(z_p)))
        y_forward(1, d)
        att_copies[i][0].wait_recv()
        part = att_all.at[x_m, pl.ds(i * SEGMENT * HD, SEGMENT * HD)]
        forwarded.append(start(part, part, xg_s.at[2, i], xg_r.at[2, i], at_x(x_p)))
    w_c.append(w_core(z_m))
    for i in range(3):
        wg[i][1].wait_recv()
    w_c.append(w_core(z_p))
    for k in range(3):
        att_copies[k][1].wait_recv()
        forwarded[k].wait_recv()

    def out_partial(dest):
        weight = w_all[dest].reshape(2 * PAD, HCOL)

        def one(j, carry):
            value = jnp.dot(weight, att_all[j], preferred_element_type=F32)
            o_part[dest, j] = value.astype(BF).reshape(2, PAD, TOK)
            return carry

        lax.fori_loop(0, 4, one, 0)

    def transpose_weight(k):
        w_t[k] = jnp.transpose(w_all[k].reshape(2 * PAD, HCOL))

    def weight_partial(dest):
        total = jnp.zeros((2 * PAD, HCOL), F32)
        for j in range(4):
            total += lax.dot_general(
                cot_all[dest, j].reshape(2 * PAD, TOK), att_all[j],
                (((1,), (1,)), ((), ())), preferred_element_type=F32,
            )
        g_part[dest] = (total * (1.0 / TOK)).astype(BF).reshape(2, PAD, HCOL)

    gc = []

    def weight_step(k, dest):
        weight_partial(dest)
        gc.append(start(g_part.at[dest, 1 - c], g_core.at[dest], gc_s.at[dest], gc_r.at[dest], sibling))

    def attended_partial(dest):
        total = jnp.zeros((HCOL, TOK), F32)
        for k in range(4):
            total += jnp.dot(w_t[k], cot_all[k, dest].reshape(2 * PAD, TOK), preferred_element_type=F32)
        a_part[dest] = total.astype(BF)

    def add_out(dest, kind, j):
        value = o_part[dest, j].astype(F32) + o_recv[kind, j].astype(F32)
        o_part[dest, j] = value.astype(BF)

    ORDER = (2, 1, 3, 0)

    yr2 = {}

    def y_middle(d):
        yr0[d].wait_recv()
        add_out(y_m, 0, (x + d) % 4)
        yr2[d] = y_copy(2, d)
        yr2[d].start()
        started.append(yr2[d])

    def weight_join(dest, i):
        rows = pl.ds(i * CHUNK, CHUNK)
        value = g_part[dest, c, rows].astype(F32) + g_core[dest, rows].astype(F32)
        return rows, value

    def z_reduce(kind, i, dest, to):
        rows = pl.ds(i * CHUNK, CHUNK)
        return start(
            g_part.at[dest, c, rows], g_recv.at[kind, rows],
            zr_s.at[kind, i], zr_r.at[kind, i], at_z(to),
        )

    def y_copy(kind, d):
        dest, to = ((y_2, y_m), (y_p, y_p), (y_m, y_m))[kind]
        j = (x + d) % 4
        return send(o_part.at[dest, j], o_recv.at[kind, j], yr_s.at[kind, d], yr_r.at[kind, d], at_y(to))

    def out_start(z):
        for kind, dest in ((0, y_2), (1, y_p)):
            @pl.when(z == dest)
            def _():
                for d in ORDER:
                    y_copy(kind, d).start()

    for i, z in enumerate((zh, z_m, z_p)):
        w_c[i].wait_recv()
        out_partial(z)
        transpose_weight(z)
    for pair in yg.values():
        pair[1].wait_recv()
    for copy in yf:
        copy.wait_recv()
    for z in (zh, z_m, z_p):
        out_start(z)
    weight_step(0, z_2)
    last = []
    for i in range(3):
        w_f[i].wait_recv()
        block = w_rows(z_2, i)
        last.append(start(block, block, wl_s.at[i], wl_r.at[i], sibling))
    weight_step(1, z_p)
    zr0 = []
    gc[0].wait_recv()
    for i in range(3):
        rows, value = weight_join(z_2, i)
        g_part[z_2, c, rows] = value.astype(BF)
        zr0.append(z_reduce(0, i, z_2, z_m))
    for copy in last:
        copy.wait_recv()
    out_partial(z_2)
    out_start(z_2)
    yr0 = {d: y_copy(0, d) for d in ORDER}
    yr1 = {d: y_copy(1, d) for d in ORDER}
    started.extend(yr0.values())
    started.extend(yr1.values())
    transpose_weight(z_2)
    attended_partial(x_2)
    ar0 = start(a_part.at[x_2], a_recv.at[0], ar_s.at[0], ar_r.at[0], at_x(x_m))
    y_middle(2)
    weight_step(2, z_m)
    gc[1].wait_recv()
    zr1 = []
    for i in range(3):
        rows, value = weight_join(z_p, i)
        g_part[z_p, c, rows] = value.astype(BF)
        zr1.append(z_reduce(1, i, z_p, z_p))
    y_middle(1)
    attended_partial(x_p)
    ar1 = start(a_part.at[x_p], a_recv.at[1], ar_s.at[1], ar_r.at[1], at_x(x_p))
    y_middle(3)
    attended_partial(x_m)
    ar0.wait_recv()
    a_part[x_m] = (a_part[x_m].astype(F32) + a_recv[0].astype(F32)).astype(BF)
    ar2 = start(a_part.at[x_m], a_recv.at[2], ar_s.at[2], ar_r.at[2], at_x(x_m))
    y_middle(0)
    gc[2].wait_recv()
    zr2 = []
    for i in range(3):
        zr0[i].wait_recv()
        rows, value = weight_join(z_m, i)
        g_part[z_m, c, rows] = (value + g_recv[0, rows].astype(F32)).astype(BF)
        zr2.append(z_reduce(2, i, z_m, z_m))
    weight_step(3, zh)
    attended_partial(x)

    def out_final(j):
        value = o_part[y, j].astype(F32) + o_recv[1, j].astype(F32) + o_recv[2, j].astype(F32)
        return value.astype(BF)

    xo = []

    def out_send(d):
        to = (x + d) % 4
        yr1[d].wait_recv()
        yr2[d].wait_recv()
        o_part[y, to] = out_final(to)
        xo.append(start(o_part.at[y, to], rx.at[x], xo_s.at[d - 1], xo_r.at[d - 1], at_x(to)))

    gkv_acc[...] = jnp.zeros_like(gkv_acc)

    def backward_head(h, carry):
        rows = pl.ds(pl.multiple_of(h * HD, HD), HD)
        grad = a_part[x, rows, :]
        soft = probs[h]
        grad_p = jnp.dot(kv[:, HD:], grad, preferred_element_type=F32)
        dot = jnp.sum(soft * grad_p, axis=0, keepdims=True)
        grad_s = (soft * (grad_p - dot) * scale).astype(BF)
        gq_o[rows, :] = jnp.dot(kv_t[:HD, :], grad_s, preferred_element_type=F32).astype(BF)
        last = (((1,), (1,)), ((), ()))
        gkv_acc[:HD, :] += lax.dot_general(q_t[rows, :], grad_s, last, preferred_element_type=F32)
        gkv_acc[HD:, :] += lax.dot_general(grad, soft.astype(BF), last, preferred_element_type=F32)
        return carry

    def backward(first, past):
        lax.fori_loop(first, past, backward_head, 0)

    out_send(2)
    ar1.wait_recv()
    ar2.wait_recv()
    a_part[x] = (
        a_part[x].astype(F32) + a_recv[1].astype(F32) + a_recv[2].astype(F32)
    ).astype(BF)
    backward(0, 4)
    out_send(1)
    out_send(3)
    backward(4, 8)
    yr1[0].wait_recv()
    yr2[0].wait_recv()
    rx[x] = out_final(x)

    def zo_send(src):
        h = src % 2
        copy = send(rx.at[src], rz.at[h], zo_s.at[h], zo_r.at[h], partner)

        @pl.when(src // 2 != zl)
        def _():
            copy.start()

    zo_send(x)
    for copy, d in zip(xo, (2, 1, 3)):
        copy.wait_recv()
        zo_send((x + 4 - d) % 4)
    backward(8, HEADS)
    gkv_o[...] = jnp.transpose(gkv_acc[...]).astype(BF)
    gc[3].wait_recv()
    for i in range(3):
        zr1[i].wait_recv()
        zr2[i].wait_recv()
        rows, value = weight_join(zh, i)
        value += g_recv[1, rows].astype(F32) + g_recv[2, rows].astype(F32)
        if i < 2:
            gw_o[rows] = value.astype(BF)
        else:
            gw_o[pl.ds(2 * CHUNK, ROWS - 2 * CHUNK)] = value[: ROWS - 2 * CHUNK].astype(BF)

    for h in range(2):
        copy = send(rx.at[2 * (1 - zl) + h], rz.at[h], zo_s.at[h], zo_r.at[h], partner)
        copy.wait_recv()
        copy.wait_send()
    value = [
        (rx[2 * zl + q // 2, q % 2].astype(F32) + rz[q // 2, q % 2].astype(F32))[:ROWS]
        for q in range(4)
    ]
    out_o[...] = jnp.concatenate(value, axis=0).astype(BF)
    for copy in started:
        copy.wait_send()


def body(queries, keys_values, out_weight, cotangent):
    vmem = pl.BlockSpec(memory_space=pltpu.VMEM)
    dma = lambda *shape: pltpu.SemaphoreType.DMA(shape)
    scratch = [
        pltpu.VMEM((2 * HD, TOK), BF),
        pltpu.VMEM((2, 2, 2, PAD, TOK), BF),
        pltpu.VMEM((4, 4, 2, PAD, TOK), BF),
        pltpu.VMEM((4, 2, PAD, HCOL), BF),
        pltpu.VMEM((4, HCOL, TOK), BF),
        pltpu.VMEM((HEADS, TOK, TOK), F32),
        pltpu.VMEM((4, HCOL, 2 * PAD), BF),
        pltpu.VMEM((4, 4, 2, PAD, TOK), BF),
        pltpu.VMEM((3, 4, 2, PAD, TOK), BF),
        pltpu.VMEM((4, 2, PAD, TOK), BF),
        pltpu.VMEM((2, 2, PAD, TOK), BF),
        pltpu.VMEM((4, 2, PAD, HCOL), BF),
        pltpu.VMEM((4, PAD, HCOL), BF),
        pltpu.VMEM((3, PAD, HCOL), BF),
        pltpu.VMEM((4, HCOL, TOK), BF),
        pltpu.VMEM((3, HCOL, TOK), BF),
        pltpu.VMEM((2 * HD, TOK), F32),
        dma(3), dma(3), dma(2), dma(2), dma(2, 3), dma(2, 3), dma(3, 2, 4), dma(3, 2, 4), dma(3, 3), dma(3, 3), dma(4), dma(4),
        dma(3, 3), dma(3, 3), dma(3, 4), dma(3, 4), dma(3), dma(3), dma(2), dma(2),
        dma(4), dma(4), dma(3, 3), dma(3, 3), dma(3), dma(3),
    ]
    out, gq, gkv, gw = pl.pallas_call(
        kernel,
        out_shape=(
            jax.ShapeDtypeStruct((4 * ROWS, TOK), BF),
            jax.ShapeDtypeStruct((HCOL, TOK), BF),
            jax.ShapeDtypeStruct((TOK, 2 * HD), BF),
            jax.ShapeDtypeStruct((ROWS, HCOL), BF),
        ),
        in_specs=[vmem] * 4,
        out_specs=(vmem,) * 4,
        scratch_shapes=scratch,
        compiler_params=pltpu.CompilerParams(
            collective_id=0, has_side_effects=True, vmem_limit_bytes=60 * 2**20
        ),
        cost_estimate=pl.CostEstimate(flops=12 * 10**9, bytes_accessed=5 * 10**6, transcendentals=10**6),
    )(queries.T, keys_values, out_weight, cotangent.T)
    return out.T, gq.T, gkv, gw


def solution(mesh):
    spec = P("dp", "tensor")
    return jax.shard_map(
        body, mesh=mesh, in_specs=(spec,) * 4, out_specs=(spec,) * 4, check_vma=False
    )
```

time: 144 us -> 117 us (0.81)
  Pallas kernels: 133 us -> 112 us
  local copies, waits for them, and re-layouts: 8.91 us -> 4.15 us
    pallas_call x1, Pallas kernels: 133 us -> 112 us  [body(): pl.pallas_call(kernel, out_shape=(jax.ShapeDtypeStruct((4 * ROWS, TOK), B...]
    pad x2 -> x0, local copies, waits for them, and re-layouts: 2.72 us -> none  [the longest x1 1.9 us: body(): w_in = jnp.pad(out_weight, ((0, PAD - ROWS), (0, 0)))]
    slice x2 -> x0, local copies, waits for them, and re-layouts: 2.69 us -> none  [the longest x1 1.89 us: body(): block_out = out[:, :ROWS].reshape(4 * ROWS, TOK).T]
    unnamed x11 -> x10, local copies, waits for them, and re-layouts: 3.5 us -> 4.15 us
where the time goes in v2:
time: 117 us; the launch traced here: 116 us
  Pallas kernels  112 us (96%)
  local copies, waits for them, and re-layouts  4.15 us (4%)
    pallas_call x1, Pallas kernels, body(): pl.pallas_call(kernel, out_shape=(jax.ShapeDtypeStruct((4 * ROWS, TOK), B...  112 us
    unnamed x10, local copies, waits for them, and re-layouts  4.15 us

profile of v2, /device:TPU:1, one launch (start us, length us, event | category | flops | bytes accessed | tf_op | source)
XLA Modules:
  0.0 116.4 jit_solution(8264069241101335956)
XLA Ops:
  0.6 111.6 %shard_map.75 = (bf16[928,256]{1,0:T(8,128)(2,1)}, bf16[960,256]{1,0:T(8,128)(2,1)}, bf16[256,128]{1,0:T(8,128)(2,1)}, bf16[232,960]{1,0:T(8,128)(2,1)}) custom-call(bf16[960,256]{1,0:T(8,128)(2,1)} %bitcast.6, bf16[256,128]{1,0:T(8,128)(2,1)} %kv.1, bf16[232,960]{1,0:T(8,128)(2,1)} %w_in.1, bf16[928,256]{1,0:T(8,128)(2,1)} %bitcast.7), custom_call_target="tpu_custom_call" | custom-call | flops 12000000000 | bytes 5000000 | tf_op jit(solution)/shard_map/pallas_call | solution.py:431
  112.2 0.0 copy-start
  112.3 1.9 %copy.12 = bf16[256,928]{0,1:T(8,128)(2,1)} copy(bf16[256,928]{0,1:T(8,128)(2,1)} %bitcast.5) | data formatting | bytes 950272
  114.1 0.0 copy-done
  114.1 0.0 copy-start.2
  114.1 0.0 copy-start.1
  114.1 0.8 copy.13
  114.9 0.1 copy-done.2
  115.0 0.6 copy.14
  115.6 0.0 copy-done.1
  115.6 0.8 copy.15
Async XLA Ops:
  112.2 1.9 %copy-start = (bf16[960,256]{1,0:T(8,128)(2,1)S(1)}, bf16[960,256]{1,0:T(8,128)(2,1)}, u32[]{:S(2)}) copy-start(bf16[960,256]{1,0:T(8,128)(2,1)} %get-tuple-element.9) | copy-start | bytes 1474564
  114.1 0.9 copy-start.2
  114.1 1.5 %copy-start.1 = (bf16[232,960]{1,0:T(8,128)(2,1)S(1)}, bf16[232,960]{1,0:T(8,128)(2,1)}, u32[]{:S(2)}) copy-start(bf16[232,960]{1,0:T(8,128)(2,1)} %get-tuple-element.19) | copy-start | bytes 1336324

commit v3 on v2

--- a/solution.py
+++ b/solution.py
@@ -142,6 +142,16 @@
             ))
         w_c.append(w_core(zh))
 
+    att_copies = []
+
+    def att_start():
+        for k in range(3):
+            part = att_all.at[x, pl.ds(k * SEGMENT * HD, SEGMENT * HD)]
+            att_copies.append((
+                start(part, part, xg_s.at[0, k], xg_r.at[0, k], at_x(x_p)),
+                start(part, part, xg_s.at[1, k], xg_r.at[1, k], at_x(x_m)),
+            ))
+
     attention_segment(0)
     attention_segment(1)
     yg, yf, xa = {}, [], {}
@@ -152,6 +162,7 @@
     zl_copy[1].wait_recv()
     xa[1] = a2a_start(1)
     w_start()
+    att_start()
     for d in (1, 3, 2):
         xa[0][d].wait_recv()
         yg[0, d] = y_start(0, d)
@@ -161,27 +172,29 @@
         xa[1][d].wait_recv()
         yg[1, d] = y_start(1, d)
         y_forward(0, d)
-    att_copies = []
-    for k in range(3):
-        part = att_all.at[x, pl.ds(k * SEGMENT * HD, SEGMENT * HD)]
-        att_copies.append((
-            start(part, part, xg_s.at[0, k], xg_r.at[0, k], at_x(x_p)),
-            start(part, part, xg_s.at[1, k], xg_r.at[1, k], at_x(x_m)),
-        ))
     y_forward(1, 0)
     w_f, forwarded = [], []
-    for i, d in enumerate((1, 3, 2)):
+
+    def w_forward(i):
         wg[i][0].wait_recv()
         block = w_rows(z_m, i)
         w_f.append(start(block, block, zg_s.at[2, i], zg_r.at[2, i], at_z(z_p)))
-        y_forward(1, d)
+
+    def att_forward(i):
         att_copies[i][0].wait_recv()
         part = att_all.at[x_m, pl.ds(i * SEGMENT * HD, SEGMENT * HD)]
         forwarded.append(start(part, part, xg_s.at[2, i], xg_r.at[2, i], at_x(x_p)))
+
+    att_forward(0)
+    w_forward(0)
+    att_forward(1)
+    y_forward(1, 1)
+    att_forward(2)
+    w_forward(1)
+    y_forward(1, 3)
+    w_forward(2)
+    y_forward(1, 2)
     w_c.append(w_core(z_m))
-    for i in range(3):
-        wg[i][1].wait_recv()
-    w_c.append(w_core(z_p))
     for k in range(3):
         att_copies[k][1].wait_recv()
         forwarded[k].wait_recv()
@@ -260,15 +273,18 @@
                     y_copy(kind, d).start()
 
     for i, z in enumerate((zh, z_m, z_p)):
+        if i == 1:
+            for k in range(3):
+                wg[k][1].wait_recv()
+            w_c.append(w_core(z_p))
         w_c[i].wait_recv()
         out_partial(z)
+        out_start(z)
         transpose_weight(z)
     for pair in yg.values():
         pair[1].wait_recv()
     for copy in yf:
         copy.wait_recv()
-    for z in (zh, z_m, z_p):
-        out_start(z)
     weight_step(0, z_2)
     last = []
     for i in range(3):

time: 117 us -> 115 us (0.983)
  Pallas kernels: 112 us -> 109 us
    pallas_call x1, Pallas kernels: 112 us -> 109 us  [body(): pl.pallas_call(kernel, out_shape=(jax.ShapeDtypeStruct((4 * ROWS, TOK), B...]
where the time goes in v3:
time: 115 us; the launch traced here: 114 us
  Pallas kernels  109 us (95%)
  local copies, waits for them, and re-layouts  4.15 us (4%)
    pallas_call x1, Pallas kernels, body(): pl.pallas_call(kernel, out_shape=(jax.ShapeDtypeStruct((4 * ROWS, TOK), B...  109 us
    unnamed x10, local copies, waits for them, and re-layouts  4.15 us

profile of v3, /device:TPU:1, one launch (start us, length us, event | category | flops | bytes accessed | tf_op | source)
XLA Modules:
  0.0 113.8 jit_solution(15770062493480256703)
XLA Ops:
  0.6 109.0 %shard_map.75 = (bf16[928,256]{1,0:T(8,128)(2,1)}, bf16[960,256]{1,0:T(8,128)(2,1)}, bf16[256,128]{1,0:T(8,128)(2,1)}, bf16[232,960]{1,0:T(8,128)(2,1)}) custom-call(bf16[960,256]{1,0:T(8,128)(2,1)} %bitcast.6, bf16[256,128]{1,0:T(8,128)(2,1)} %kv.1, bf16[232,960]{1,0:T(8,128)(2,1)} %w_in.1, bf16[928,256]{1,0:T(8,128)(2,1)} %bitcast.7), custom_call_target="tpu_custom_call" | custom-call | flops 12000000000 | bytes 5000000 | tf_op jit(solution)/shard_map/pallas_call | solution.py:447
  109.7 0.0 copy-start
  109.7 1.9 %copy.12 = bf16[256,928]{0,1:T(8,128)(2,1)} copy(bf16[256,928]{0,1:T(8,128)(2,1)} %bitcast.5) | data formatting | bytes 950272
  111.6 0.0 copy-done
  111.6 0.0 copy-start.2
  111.6 0.0 copy-start.1
  111.6 0.8 copy.13
  112.4 0.1 copy-done.2
  112.4 0.6 copy.14
  113.1 0.0 copy-done.1
  113.1 0.8 copy.15
Async XLA Ops:
  109.7 1.9 %copy-start = (bf16[960,256]{1,0:T(8,128)(2,1)S(1)}, bf16[960,256]{1,0:T(8,128)(2,1)}, u32[]{:S(2)}) copy-start(bf16[960,256]{1,0:T(8,128)(2,1)} %get-tuple-element.9) | copy-start | bytes 1474564
  111.6 0.9 copy-start.2
  111.6 1.5 %copy-start.1 = (bf16[232,960]{1,0:T(8,128)(2,1)S(1)}, bf16[232,960]{1,0:T(8,128)(2,1)}, u32[]{:S(2)}) copy-start(bf16[232,960]{1,0:T(8,128)(2,1)} %get-tuple-element.19) | copy-start | bytes 1336324

commit v4 on v3

--- a/solution.py
+++ b/solution.py
@@ -280,6 +280,7 @@
         w_c[i].wait_recv()
         out_partial(z)
         out_start(z)
+    for z in (zh, z_m, z_p):
         transpose_weight(z)
     for pair in yg.values():
         pair[1].wait_recv()

time: 115 us -> 114 us (level)
  no operation moved by 1% of the time
where the time goes in v4:
time: 114 us
  Pallas kernels  109 us (96%)
  local copies, waits for them, and re-layouts  4.15 us (4%)
    pallas_call x1, Pallas kernels, body(): pl.pallas_call(kernel, out_shape=(jax.ShapeDtypeStruct((4 * ROWS, TOK), B...  109 us
    unnamed x10, local copies, waits for them, and re-layouts  4.15 us

profile of v4, /device:TPU:1, one launch (start us, length us, event | category | flops | bytes accessed | tf_op | source)
XLA Modules:
  0.0 113.8 jit_solution(7027690264002779098)
XLA Ops:
  0.6 109.0 %shard_map.75 = (bf16[928,256]{1,0:T(8,128)(2,1)}, bf16[960,256]{1,0:T(8,128)(2,1)}, bf16[256,128]{1,0:T(8,128)(2,1)}, bf16[232,960]{1,0:T(8,128)(2,1)}) custom-call(bf16[960,256]{1,0:T(8,128)(2,1)} %bitcast.6, bf16[256,128]{1,0:T(8,128)(2,1)} %kv.1, bf16[232,960]{1,0:T(8,128)(2,1)} %w_in.1, bf16[928,256]{1,0:T(8,128)(2,1)} %bitcast.7), custom_call_target="tpu_custom_call" | custom-call | flops 12000000000 | bytes 5000000 | tf_op jit(solution)/shard_map/pallas_call | solution.py:448
  109.6 0.0 copy-start
  109.6 1.9 %copy.12 = bf16[256,928]{0,1:T(8,128)(2,1)} copy(bf16[256,928]{0,1:T(8,128)(2,1)} %bitcast.5) | data formatting | bytes 950272
  111.5 0.0 copy-done
  111.5 0.0 copy-start.2
  111.5 0.0 copy-start.1
  111.5 0.8 copy.13
  112.3 0.1 copy-done.2
  112.4 0.6 copy.14
  113.0 0.0 copy-done.1
  113.0 0.8 copy.15
Async XLA Ops:
  109.6 1.9 %copy-start = (bf16[960,256]{1,0:T(8,128)(2,1)S(1)}, bf16[960,256]{1,0:T(8,128)(2,1)}, u32[]{:S(2)}) copy-start(bf16[960,256]{1,0:T(8,128)(2,1)} %get-tuple-element.9) | copy-start | bytes 1474564
  111.5 0.9 copy-start.2
  111.5 1.5 %copy-start.1 = (bf16[232,960]{1,0:T(8,128)(2,1)S(1)}, bf16[232,960]{1,0:T(8,128)(2,1)}, u32[]{:S(2)}) copy-start(bf16[232,960]{1,0:T(8,128)(2,1)} %get-tuple-element.19) | copy-start | bytes 1336324
